TPU v7x, 32 devices: a whole 2x2x4 slice. The times are simulated.
32 devices in a mesh: group: 4 (over y, core), within: 8 (over z, x).
Axes of the slice: x: 2, y: 2, z: 4, core: 2. Of those that a mesh axis runs over, the one named last changes fastest.
Arguments:
- tokens: bfloat16 [4096, 2048], P(('group', 'within')), may hold values from -6 to 6
- languages: int32 [4096], P(('group', 'within')), may hold values from 0 to 99, as said below
- lang_group: int32 [100], replicated, may hold values from 0 to 3, as said below
- group_gain: float32 [4, 2048], replicated, may hold values from 0.25 to 1.75
- group_w1: bfloat16 [4, 2048, 8192], P('group', None, 'within'), may hold values from -0.125 to 0.125
- group_b1: float32 [4, 8192], P('group', 'within'), may hold values from -3 to 3
- group_w2: bfloat16 [4, 8192, 2048], P('group', 'within'), may hold values from -0.0625 to 0.0625
- group_b2: float32 [4, 2048], replicated, may hold values from -3 to 3
- shared_gain: float32 [2048], replicated, may hold values from 0.25 to 1.75
- shared_w1: bfloat16 [2048, 8192], P(None, 'group'), may hold values from -0.125 to 0.125
- shared_b1: float32 [8192], P('group'), may hold values from -3 to 3
- shared_w2: bfloat16 [8192, 2048], P('group'), may hold values from -0.0625 to 0.0625
- shared_b2: float32 [2048], replicated, may hold values from -3 to 3
Outputs:
- encoded: bfloat16 [4096, 2048], P(('group', 'within'))
Inputs may be any that keep to these rules, and one draw needn't show every extreme that they name: `lang_group`: every language lies in one group and every group holds at least one language. Among the 128 tokens of one device (an aligned block), at most 48 have languages of one group, and in every block some group has exactly 48.
All inputs are finite; a program needn't handle non-finite values.
Results may differ from a plain program's by a relative error of at most 0.017.
Values may be sent and summed in bfloat16 or wider, within the bound.
A program may use at most 128 MiB of HBM per device.

v0:
```python
import jax
import jax.numpy as jnp
from jax import lax
from jax.sharding import PartitionSpec as P


def layer_norm(values, gains):
    centre = jnp.mean(values, axis=-1, keepdims=True)
    centred = values - centre
    spread = jnp.mean(centred * centred, axis=-1, keepdims=True)
    return centred * lax.rsqrt(spread + 1e-05) * gains


def on_device(
    tokens,
    languages,
    lang_group,
    group_gain,
    group_w1,
    group_b1,
    group_w2,
    group_b2,
    shared_gain,
    shared_w1,
    shared_b1,
    shared_w2,
    shared_b2,
):
    tok_dev = tokens.shape[0]
    width_model = tokens.shape[1]
    num_groups = group_gain.shape[0]
    num_langs = lang_group.shape[0]
    capacity = 3 * tok_dev // (2 * lax.axis_size("group"))
    residual_in = tokens.astype(jnp.float32)
    lang_hit = (languages[:, None] == jnp.arange(num_langs, dtype=jnp.int32)[None, :]).astype(
        jnp.int32
    )
    group_of = jnp.sum(lang_hit * lang_group[None, :], axis=1)
    onehot = (group_of[:, None] == jnp.arange(num_groups, dtype=jnp.int32)[None, :]).astype(
        jnp.int32
    )
    earlier = jnp.cumsum(onehot, axis=0) - onehot
    slot_index = jnp.sum(earlier * onehot, axis=1)
    position = group_of * capacity + slot_index
    dispatch_map = (
        position[None, :] == jnp.arange(num_groups * capacity, dtype=jnp.int32)[:, None]
    ).astype(jnp.bfloat16)
    onehot_float = onehot.astype(jnp.float32)
    row_gains = jnp.dot(onehot_float, group_gain, precision=lax.Precision.HIGHEST)
    normed = layer_norm(residual_in, row_gains).astype(jnp.bfloat16)
    outgoing = jnp.dot(dispatch_map, normed, preferred_element_type=jnp.float32).astype(
        jnp.bfloat16
    )
    outgoing = outgoing.reshape(num_groups, capacity, width_model)
    arrived = lax.all_to_all(outgoing, "group", split_axis=0, concat_axis=0, tiled=True)
    group_rows = arrived.reshape(num_groups * capacity, width_model)
    first_proj = group_w1[0]
    first_bias = group_b1[0]
    second_proj = group_w2[0]
    hidden = jax.nn.relu(
        jnp.dot(
            lax.all_gather(group_rows, "within", axis=0, tiled=True),
            first_proj,
            preferred_element_type=jnp.float32,
        )
        + first_bias
    ).astype(jnp.bfloat16)
    selected = hidden
    summed = lax.psum_scatter(
        jnp.dot(selected, second_proj, preferred_element_type=jnp.float32).astype(jnp.bfloat16),
        "within",
        scatter_dimension=0,
        tiled=True,
    )
    returned = lax.all_to_all(
        summed.reshape(num_groups, capacity, width_model),
        "group",
        split_axis=0,
        concat_axis=0,
        tiled=True,
    )
    returned = returned.reshape(num_groups * capacity, width_model)
    group_out = lax.dot_general(
        dispatch_map, returned, (((0,), (0,)), ((), ())), preferred_element_type=jnp.float32
    )
    group_bias = jnp.dot(onehot_float, group_b2, precision=lax.Precision.HIGHEST)
    middle = residual_in + group_out + group_bias
    shared_in = layer_norm(middle, shared_gain).astype(jnp.bfloat16)
    shared_hidden = jax.nn.relu(
        jnp.dot(
            lax.all_gather(shared_in, "group", axis=0, tiled=True),
            shared_w1,
            preferred_element_type=jnp.float32,
        )
        + shared_b1
    ).astype(jnp.bfloat16)
    selected = shared_hidden
    shared_out = lax.psum_scatter(
        jnp.dot(selected, shared_w2, preferred_element_type=jnp.float32).astype(jnp.bfloat16),
        "group",
        scatter_dimension=0,
        tiled=True,
    ).astype(jnp.float32)
    return (middle + shared_out + shared_b2).astype(jnp.bfloat16)


def solution(mesh):
    placed = (
        P(("group", "within"), None),
        P(("group", "within")),
        P(),
        P(),
        P("group", None, "within"),
        P("group", "within"),
        P("group", "within", None),
        P(),
        P(),
        P(None, "group"),
        P("group"),
        P("group", None),
        P(),
    )
    return jax.shard_map(
        on_device,
        mesh=mesh,
        in_specs=placed,
        out_specs=P(("group", "within"), None),
        check_vma=False,
    )
```

profile of v0, /device:TPU:0, one launch (start us, length us, event | category | flops | bytes accessed | tf_op | source)
XLA Modules:
  0.0 359.7 jit_solution(5469800090780039300)
XLA Ops:
  6.5 0.0 copy-start
  6.5 0.0 copy-start.5
  6.5 0.0 all-gather.3.cloned.1.call-start
  6.5 1.2 convert_reduce_fusion
  7.8 1.3 fusion.9
  9.1 0.8 select_reduce_fusion
  9.9 0.1 fusion.16
  10.0 0.2 reduce_window_sum.11
  10.1 0.2 fusion.15
  10.3 2.1 fusion.6
  12.5 0.4 convolution_convert_fusion.2
  12.8 15.8 %all_to_all.10 = bf16[4,48,2048]{2,1,0:T(8,128)(2,1)} all-to-all(bf16[4,48,2048]{2,1,0:T(8,128)(2,1)S(1)} %bitcast.23), channel_id=1, replica_groups=mesh['group'=4,'within'=8] {'group'}, dimensions={0} | all-to-all | bytes 1572864 | tf_op jit(solution)/shard_map/all_to_all | solution.py:55
  28.6 0.0 all-gather.3.cloned.1.call-update
  28.7 0.0 reduce-scatter.3.cloned.1.call-start
  28.7 99.8 %all-gather.3.cloned.1.call-done = bf16[1536,2048]{1,0:T(8,128)(2,1)} async-done(((bf16[192,2048]{1,0:T(8,128)(2,1)}), bf16[1536,2048]{1,0:T(8,128)(2,1)}) %all-gather.3.cloned.1.call-update) | async-done | bytes 6291472 | tf_op jit(solution)/shard_map/all_gather | solution.py:62
  128.6 0.0 copy-done.5
  128.6 19.3 %convolution_convert_fusion = bf16[1536,2048]{1,0:T(8,128)(2,1)} fusion(bf16[1,1024,2048]{2,1,0:T(8,128)(2,1)} %param.19, bf16[1536,2048]{1,0:T(8,128)(2,1)} %all-gather.3.cloned.1.call-done, bf16[1,2048,1024]{2,1,0:T(8,128)(2,1)} %param.17, f32[1024]{0:T(1024)S(1)} %bitcast.25), kind=kOutput, calls=%fused_computation | convolution fusion | flops 12892766208 | bytes 20975616 | tf_op jit(solution)/shard_map/dot_general | solution.py:70
  147.9 0.0 copy-start.1
  147.9 0.0 reduce-scatter.3.cloned.1.call-update
  147.9 0.0 copy-start.2
  147.9 0.0 all-gather.5.cloned.1.call-start
  147.9 116.2 %reduce-scatter.3.cloned.1.call-done = bf16[192,2048]{1,0:T(8,128)(2,1)} async-done(((bf16[1536,2048]{1,0:T(8,128)(2,1)}), bf16[192,2048]{1,0:T(8,128)(2,1)}) %reduce-scatter.3.cloned.1.call-update) | async-done | bytes 786448 | tf_op jit(solution)/shard_map/reduce_scatter | solution.py:69
  264.2 15.1 %all_to_all.11 = bf16[4,48,2048]{2,1,0:T(8,128)(2,1)S(1)} all-to-all(bf16[4,48,2048]{2,1,0:T(8,128)(2,1)} %bitcast.24), channel_id=1, replica_groups=mesh['group'=4,'within'=8] {'group'}, dimensions={0} | all-to-all | bytes 1572864 | tf_op jit(solution)/shard_map/all_to_all | solution.py:75
  279.3 0.0 copy-start.4
  279.3 0.0 copy-done.1
  279.3 0.4 convolution_add_fusion.1
  279.6 0.0 copy-done
  279.6 1.1 fusion.23
  280.8 0.3 multiply_reduce_fusion
  281.1 0.0 copy-done.2
  281.1 1.0 multiply_convert_fusion
  282.1 0.0 all-gather.5.cloned.1.call-update
  282.1 0.0 copy-start.3
  282.1 0.2 reduce-scatter.5.cloned.1.call-start
  282.3 20.7 %all-gather.5.cloned.1.call-done = bf16[512,2048]{1,0:T(8,128)(2,1)} async-done(((bf16[128,2048]{1,0:T(8,128)(2,1)}), bf16[512,2048]{1,0:T(8,128)(2,1)}) %all-gather.5.cloned.1.call-update) | async-done | bytes 2097168 | tf_op jit(solution)/shard_map/all_gather | solution.py:91
  303.1 0.0 copy-done.4
  303.1 16.5 %convolution_convert_fusion.1 = bf16[512,2048]{1,0:T(8,128)(2,1)} fusion(bf16[2048,2048]{1,0:T(8,128)(2,1)} %param.24, bf16[512,2048]{1,0:T(8,128)(2,1)} %all-gather.5.cloned.1.call-done, bf16[2048,2048]{1,0:T(8,128)(2,1)} %param.22, f32[2048]{0:T(1024)S(1)} %copy-done.4), kind=kOutput, calls=%fused_computation.7 | convolution fusion | flops 8594128896 | bytes 20979712 | tf_op jit(solution)/shard_map/dot_general | solution.py:99
  319.6 0.0 reduce-scatter.5.cloned.1.call-update
  319.6 31.6 %reduce-scatter.5.cloned.1.call-done = bf16[128,2048]{1,0:T(8,128)(2,1)} async-done(((bf16[512,2048]{1,0:T(8,128)(2,1)}), bf16[128,2048]{1,0:T(8,128)(2,1)}) %reduce-scatter.5.cloned.1.call-update) | async-done | bytes 524304 | tf_op jit(solution)/shard_map/reduce_scatter | solution.py:98
  351.2 0.0 copy-done.3
  351.2 2.0 add_convert_fusion
  (5 shorter events, 0.0 us)
Async XLA Ops:
  6.5 273.1 %copy-start = (f32[4,2048]{1,0:T(4,128)S(1)}, f32[4,2048]{1,0:T(4,128)}, u32[]{:S(2)}) copy-start(f32[4,2048]{1,0:T(4,128)} %param.20) | copy-start | bytes 98308
  6.5 122.0 %copy-start.5 = (f32[1,1024]{1,0:T(1,128)S(1)}, f32[1,1024]{1,0:T(1,128)}, u32[]{:S(2)}) copy-start(f32[1,1024]{1,0:T(1,128)} %param.18) | copy-start | bytes 12292
  6.5 122.0 %all-gather.3.cloned.1.call-start = ((), (), s32[]{:S(2)}) async-start(), calls=%async_computation.4 | async-start | bytes 7077888 | tf_op jit(solution)/shard_map/all_gather | solution.py:62
  28.7 235.5 %reduce-scatter.3.cloned.1.call-start = ((), (), s32[]{:S(2)}) async-start(), calls=%async_computation.5 | async-start | bytes 7077888 | tf_op jit(solution)/shard_map/reduce_scatter | solution.py:69
  147.9 131.4 %copy-start.1 = (bf16[128,2048]{1,0:T(8,128)(2,1)S(1)}, bf16[128,2048]{1,0:T(8,128)(2,1)}, u32[]{:S(2)}) copy-start(bf16[128,2048]{1,0:T(8,128)(2,1)} %param.13) | copy-start | bytes 1572868
  147.9 133.2 %copy-start.2 = (f32[2048]{0:T(1024)S(1)}, f32[2048]{0:T(1024)}, u32[]{:S(2)}) copy-start(f32[2048]{0:T(1024)} %param.21) | copy-start | bytes 24580
  147.9 155.2 %all-gather.5.cloned.1.call-start = ((), (), s32[]{:S(2)}) async-start(), calls=%async_computation.6 | async-start | bytes 2621440 | tf_op jit(solution)/shard_map/all_gather | solution.py:91
  279.3 23.8 %copy-start.4 = (f32[2048]{0:T(1024)S(1)}, f32[2048]{0:T(1024)}, u32[]{:S(2)}) copy-start(f32[2048]{0:T(1024)} %param.23) | copy-start | bytes 24580
  282.1 69.1 %copy-start.3 = (f32[2048]{0:T(1024)S(1)}, f32[2048]{0:T(1024)}, u32[]{:S(2)}) copy-start(f32[2048]{0:T(1024)} %param.25) | copy-start | bytes 24580
  282.1 69.1 %reduce-scatter.5.cloned.1.call-start = ((), (), s32[]{:S(2)}) async-start(), calls=%async_computation.7 | async-start | bytes 2621440 | tf_op jit(solution)/shard_map/reduce_scatter | solution.py:98
Sparse Core Ops, SparseCore 0:
  28.8 99.7 all-gather.2
  148.0 116.1 reduce-scatter.2
  282.2 20.8 all-gather.4
  319.8 31.4 reduce-scatter.4
where the time goes:
time: 360 us
  waiting for transfers between devices  268 us (74%)
  matrix products  39.8 us (11%)
  blocking collectives  30.9 us (9%)
  between operations  13.2 us (4%)
  other arithmetic  7.03 us (2%)
    reduce_scatter x1, waiting for transfers between devices, on_device(): lax.psum_scatter(jnp.dot(selected, second_proj, preferred_element_type=jn...  116 us
    all_gather x1, waiting for transfers between devices, on_device(): lax.all_gather(group_rows, 'within', axis=0, tiled=True)  99.8 us
    reduce_scatter x1, waiting for transfers between devices, on_device(): lax.psum_scatter(jnp.dot(selected, shared_w2, preferred_element_type=jnp....  31.6 us
    all_gather x1, waiting for transfers between devices, on_device(): lax.all_gather(shared_in, 'group', axis=0, tiled=True)  20.7 us
    dot_general x1, matrix products, on_device(): jnp.dot(selected, second_proj, preferred_element_type=jnp.float32)  19.3 us
    dot_general x1, matrix products, on_device(): jnp.dot(selected, shared_w2, preferred_element_type=jnp.float32)  16.5 us
    all_to_all x1, blocking collectives, on_device(): lax.all_to_all(outgoing, 'group', split_axis=0, concat_axis=0, tiled=True)  15.8 us
    all_to_all x1, blocking collectives, on_device(): lax.all_to_all(summed.reshape(num_groups, capacity, width_model), 'group'...  15.1 us
  transfers between devices with their start and end apart: 4, of which 4 were waited for; matrix products, arithmetic and copies ran while one was open for 0% of the time, Pallas kernels for 0%

commit v1 on v0

--- a/solution.py
+++ b/solution.py
@@ -1,7 +1,14 @@
+import functools
+
 import jax
 import jax.numpy as jnp
 from jax import lax
+from jax.experimental import pallas as pl
+from jax.experimental.pallas import tpu as pltpu
 from jax.sharding import PartitionSpec as P
+
+MESH = pl.DeviceIdType.MESH
+TILE = 256
 
 
 def layer_norm(values, gains):
@@ -11,7 +18,507 @@
     return centred * lax.rsqrt(spread + 1e-05) * gains
 
 
-def on_device(
+def columns(tile, size):
+    return pl.ds(pl.multiple_of(tile * size, size), size)
+
+
+def fused_kernel(
+    cap,
+    out_rows,
+    back_map,
+    residual,
+    b1,
+    gain2,
+    sb1,
+    sb2,
+    w1_hbm,
+    w2_hbm,
+    sw1_hbm,
+    sw2_hbm,
+    encoded,
+    w1,
+    w2,
+    sw1,
+    sw2,
+    rows,
+    part,
+    rs,
+    hidden,
+    ret,
+    sgather,
+    shidden,
+    spart,
+    sown,
+    scross,
+    ssum,
+    middle,
+    w_sem,
+    local_sem,
+    disp_send,
+    disp_recv,
+    g_send,
+    g_recv,
+    r_send,
+    r_recv,
+    ret_send,
+    ret_recv,
+    sg_send,
+    sg_recv,
+    sr_send,
+    sr_recv,
+):
+    g = lax.axis_index("group")
+    w = lax.axis_index("within")
+    last = 7
+    x, z = lax.rem(w, 2), lax.div(w, 2)
+    p = z + x * (last - 2 * z)
+
+    def device_at(q):
+        q = lax.rem(q + 8, 8)
+        far = lax.div(q, 4)
+        return 2 * q + far * (15 - 4 * q)
+
+    right = (g, device_at(p + 1))
+    left = (g, device_at(p - 1))
+    yy, core = lax.div(g, 2), lax.rem(g, 2)
+    peers = [
+        None,
+        (2 * yy + 1 - core, w),
+        (2 * (1 - yy) + core, w),
+        (2 * (1 - yy) + 1 - core, w),
+    ]
+
+    loads = []
+    for i, (src, dst) in enumerate(
+        ((w1_hbm, w1), (w2_hbm, w2), (sw1_hbm, sw1), (sw2_hbm, sw2))
+    ):
+        copy = pltpu.make_async_copy(src, dst, w_sem.at[i])
+        copy.start()
+        loads.append(copy)
+    own = pltpu.make_async_copy(
+        out_rows.at[pl.ds(0, cap)], rows.at[pl.ds(0, cap)], local_sem
+    )
+    own.start()
+
+    barrier = pltpu.get_barrier_semaphore()
+    for device in (right, left, peers[1], peers[2], peers[3]):
+        pl.semaphore_signal(barrier, inc=1, device_id=device, device_id_type=MESH)
+    pl.semaphore_wait(barrier, 5)
+
+    pending = []
+
+    def send(src, dst, send_sem, recv_sem, device):
+        copy = pltpu.make_async_remote_copy(
+            src_ref=src,
+            dst_ref=dst,
+            send_sem=send_sem,
+            recv_sem=recv_sem,
+            device_id=device,
+            device_id_type=MESH,
+        )
+        copy.start()
+        pending.append(copy)
+        return copy
+
+    def chunk(slot, c):
+        return pl.ds((slot * 4 + c) * cap, cap)
+
+    dispatch = [None] * 4
+    for r in (2, 3, 1):
+        dispatch[r] = send(
+            out_rows.at[pl.ds(r * cap, cap)],
+            rows.at[chunk(0, r)],
+            disp_send.at[r],
+            disp_recv.at[r],
+            peers[r],
+        )
+
+    def slot_of(way, s):
+        return 7 if s == 4 else (0 if s == 0 else 2 * s - 1 + way)
+
+    arrivals = {}
+
+    def forward(way, s, c):
+        slot = slot_of(way, s)
+        arrivals[way, s + 1, c] = send(
+            rows.at[chunk(slot, c)],
+            rows.at[chunk(slot_of(way, s + 1), c)],
+            g_send.at[way, s, c],
+            g_recv.at[way, s + 1, c],
+            right if way == 0 else left,
+        )
+
+    def first_tiles(slot, count, begin, end):
+        size = count * 4 * cap
+
+        def body(i, carry):
+            cols = columns(i, TILE)
+            value = jnp.dot(
+                rows[pl.ds(slot * 4 * cap, size), :],
+                w1[:, cols],
+                preferred_element_type=jnp.float32,
+            )
+            hidden[pl.ds(0, size), cols] = jnp.maximum(value + b1[:, cols], 0.0).astype(
+                jnp.bfloat16
+            )
+            return carry
+
+        lax.fori_loop(begin, end, body, 0)
+
+    def second_tiles(slot, count, begin, end):
+        size = count * 4 * cap
+
+        def body(i, carry):
+            cols = columns(i, TILE)
+            part[pl.ds(slot * 4 * cap, size), cols] = jnp.dot(
+                hidden[pl.ds(0, size), :],
+                w2[:, cols],
+                preferred_element_type=jnp.float32,
+            ).astype(jnp.bfloat16)
+            return carry
+
+        lax.fori_loop(begin, end, body, 0)
+
+    n1, n2 = w1.shape[1] // TILE, w2.shape[1] // TILE
+
+    def piece(slot, count, c):
+        if c < 2:
+            first_tiles(slot, count, c * n1 // 2, (c + 1) * n1 // 2)
+        else:
+            second_tiles(slot, count, (c - 2) * n2 // 2, (c - 1) * n2 // 2)
+
+    own.wait()
+    for c in range(4):
+        if c:
+            dispatch[c].wait_recv()
+        forward(0, 0, c)
+        forward(1, 0, c)
+    loads[0].wait()
+    loads[1].wait()
+    for s in (1, 2, 3):
+        for c in range(4):
+            for way in (0, 1):
+                arrivals[way, s, c].wait_recv()
+                if s < 3 or c // 2 == way:
+                    forward(way, s, c)
+            if s == 1:
+                piece(0, 1, c)
+            else:
+                piece(2 * s - 3, 2, c)
+    for c in range(4):
+        piece(5, 2, c)
+
+    def rs_slot(way, t):
+        return (7, 6 - way, 4 - way, 2 - way)[t]
+
+    def rs_chunk(way, t, c):
+        place = way * 14 + (c % 2 if t == 0 else 4 * t - 2 + c)
+        return pl.ds(place * cap, cap)
+
+    sums = {}
+
+    def pass_on(way, t, c):
+        sums[way, t, c] = send(
+            part.at[chunk(rs_slot(way, t), c)],
+            rs.at[rs_chunk(way, t, c)],
+            r_send.at[way, t, c],
+            r_recv.at[way, t, c],
+            right if way == 0 else left,
+        )
+
+    def add_in(way, t, c):
+        sums[way, t, c].wait_recv()
+        here = chunk(rs_slot(way, t + 1), c)
+        part[here, :] = (
+            part[here, :].astype(jnp.float32)
+            + rs[rs_chunk(way, t, c), :].astype(jnp.float32)
+        ).astype(jnp.bfloat16)
+
+    for c in (2, 3):
+        pass_on(0, 1, c)
+        pass_on(1, 1, c - 2)
+    for c in (0, 1):
+        arrivals[0, 4, c].wait_recv()
+        arrivals[1, 4, c + 2].wait_recv()
+    for c in range(4):
+        piece(7, 1, c)
+    for c in (0, 1):
+        pass_on(0, 0, c)
+        pass_on(1, 0, c + 2)
+    for c in (0, 1):
+        add_in(0, 0, c)
+        pass_on(0, 1, c)
+        add_in(1, 0, c + 2)
+        pass_on(1, 1, c + 2)
+    order = (2, 3, 0, 1)
+    for t in (1, 2):
+        for c in order:
+            for way in (0, 1):
+                add_in(way, t, c)
+                pass_on(way, t + 1, c)
+
+    returned = [None] * 4
+    for c in order:
+        sums[0, 3, c].wait_recv()
+        sums[1, 3, c].wait_recv()
+        here = chunk(0, c)
+        total = (
+            part[here, :].astype(jnp.float32)
+            + rs[rs_chunk(0, 3, c), :].astype(jnp.float32)
+            + rs[rs_chunk(1, 3, c), :].astype(jnp.float32)
+        ).astype(jnp.bfloat16)
+        if c == 0:
+            ret[pl.ds(0, cap), :] = total
+        else:
+            part[here, :] = total
+            returned[c] = send(
+                part.at[here],
+                ret.at[pl.ds(c * cap, cap)],
+                ret_send.at[c],
+                ret_recv.at[c],
+                peers[c],
+            )
+    for c in (1, 2, 3):
+        returned[c].wait_recv()
+
+    tokens = residual.shape[0]
+    half = tokens // 2
+
+    def block(r, h=None):
+        if h is None:
+            return pl.ds(r * tokens, tokens)
+        return pl.ds(r * tokens + h * half, half)
+
+    from_sibling, from_y, from_far = [], [], []
+    for h in range(2):
+        some = pl.ds(h * half, half)
+        group_out = jnp.dot(
+            back_map[some, :], ret[...], preferred_element_type=jnp.float32
+        )
+        value = residual[some, :] + group_out
+        middle[some, :] = value
+        sgather[some, :] = layer_norm(value, gain2[...]).astype(jnp.bfloat16)
+        from_y.append(
+            send(
+                sgather.at[some],
+                sgather.at[block(2, h)],
+                sg_send.at[0, h],
+                sg_recv.at[0, h],
+                peers[2],
+            )
+        )
+        from_sibling.append(
+            send(
+                sgather.at[some],
+                sgather.at[block(1, h)],
+                sg_send.at[1, h],
+                sg_recv.at[1, h],
+                peers[1],
+            )
+        )
+
+    m1, m2 = sw1.shape[1] // TILE, sw2.shape[1] // TILE
+
+    def shared_first(pair):
+        def body(i, carry):
+            cols = columns(i, TILE)
+            value = jnp.dot(
+                sgather[pl.ds(pair * 2 * tokens, 2 * tokens), :],
+                sw1[:, cols],
+                preferred_element_type=jnp.float32,
+            )
+            shidden[:, cols] = jnp.maximum(value + sb1[:, cols], 0.0).astype(jnp.bfloat16)
+            return carry
+
+        lax.fori_loop(0, m1, body, 0)
+
+    def shared_second(pair, begin, end):
+        def body(i, carry):
+            cols = columns(i, TILE)
+            spart[pl.ds(pair * 2 * tokens, 2 * tokens), cols] = jnp.dot(
+                shidden[...], sw2[:, cols], preferred_element_type=jnp.float32
+            ).astype(jnp.bfloat16)
+            return carry
+
+        lax.fori_loop(begin, end, body, 0)
+
+    loads[2].wait()
+    loads[3].wait()
+    for h in range(2):
+        from_sibling[h].wait_recv()
+    shared_first(0)
+    for h in range(2):
+        from_y[h].wait_recv()
+        from_far.append(
+            send(
+                sgather.at[block(2, h)],
+                sgather.at[block(3, h)],
+                sg_send.at[2, h],
+                sg_recv.at[2, h],
+                peers[1],
+            )
+        )
+    shared_second(0, 0, m2)
+    to_own = send(
+        spart.at[block(1)], sown, sr_send.at[2, 0], sr_recv.at[2, 0], peers[1]
+    )
+    for h in range(2):
+        from_far[h].wait_recv()
+    shared_first(1)
+    quarters = 4
+    width = sw2.shape[1] // quarters
+    crossed, summed = [], []
+
+    def finish_quarter(q):
+        cols = pl.ds(q * width, width)
+        crossed[q].wait_recv()
+        spart[block(2), cols] = (
+            spart[block(2), cols].astype(jnp.float32) + scross[:, cols].astype(jnp.float32)
+        ).astype(jnp.bfloat16)
+        summed.append(
+            send(
+                spart.at[block(2), cols],
+                ssum.at[:, cols],
+                sr_send.at[1, q],
+                sr_recv.at[1, q],
+                peers[2],
+            )
+        )
+
+    for q in range(quarters):
+        cols = pl.ds(q * width, width)
+        shared_second(1, q * m2 // quarters, (q + 1) * m2 // quarters)
+        crossed.append(
+            send(
+                spart.at[block(3), cols],
+                scross.at[:, cols],
+                sr_send.at[0, q],
+                sr_recv.at[0, q],
+                peers[1],
+            )
+        )
+        if q:
+            finish_quarter(q - 1)
+    finish_quarter(quarters - 1)
+    to_own.wait_recv()
+    for q in range(quarters):
+        cols = pl.ds(q * width, width)
+        summed[q].wait_recv()
+        encoded[:, cols] = (
+            middle[:, cols]
+            + (
+                spart[block(0), cols].astype(jnp.float32)
+                + sown[:, cols].astype(jnp.float32)
+                + ssum[:, cols].astype(jnp.float32)
+            )
+            + sb2[:, cols]
+        ).astype(jnp.bfloat16)
+    for copy in pending:
+        copy.wait_send()
+
+
+def fused_on_device(
+    tokens,
+    languages,
+    lang_group,
+    group_gain,
+    group_w1,
+    group_b1,
+    group_w2,
+    group_b2,
+    shared_gain,
+    shared_w1,
+    shared_b1,
+    shared_w2,
+    shared_b2,
+):
+    tok_dev, width = tokens.shape
+    num_groups = group_gain.shape[0]
+    num_langs = lang_group.shape[0]
+    cap = 3 * tok_dev // (2 * num_groups)
+    me = lax.axis_index("group")
+    residual = tokens.astype(jnp.float32)
+    lang_hit = languages[:, None] == jnp.arange(num_langs, dtype=jnp.int32)[None, :]
+    group_of = jnp.sum(jnp.where(lang_hit, lang_group[None, :], 0), axis=1)
+    onehot = group_of[:, None] == jnp.arange(num_groups, dtype=jnp.int32)[None, :]
+    same = group_of[:, None] == group_of[None, :]
+    index = jnp.arange(tok_dev, dtype=jnp.int32)
+    before = index[None, :] < index[:, None]
+    slot_index = jnp.sum((same & before).astype(jnp.int32), axis=1)
+    position = (group_of ^ me) * cap + slot_index
+    slots = jnp.arange(num_groups * cap, dtype=jnp.int32)
+    out_map = (position[None, :] == slots[:, None]).astype(jnp.bfloat16)
+    back_map = (position[:, None] == slots[None, :]).astype(jnp.bfloat16)
+    onehot_float = onehot.astype(jnp.float32)
+    row_gains = jnp.dot(onehot_float, group_gain, precision=lax.Precision.HIGHEST)
+    normed = layer_norm(residual, row_gains).astype(jnp.bfloat16)
+    outgoing = jnp.dot(out_map, normed, preferred_element_type=jnp.float32).astype(
+        jnp.bfloat16
+    )
+    group_bias = jnp.dot(onehot_float, group_b2, precision=lax.Precision.HIGHEST)
+    unit = group_w1.shape[2]
+    shared_unit = shared_w1.shape[1]
+    rows = num_groups * cap
+    bf16, f32 = jnp.bfloat16, jnp.float32
+    in_vmem = pl.BlockSpec(memory_space=pltpu.VMEM)
+    anywhere = pl.BlockSpec(memory_space=pl.ANY)
+    dma = pltpu.SemaphoreType.DMA
+    return pl.pallas_call(
+        functools.partial(fused_kernel, cap),
+        out_shape=jax.ShapeDtypeStruct((tok_dev, width), bf16),
+        in_specs=[in_vmem] * 7 + [anywhere] * 4,
+        out_specs=in_vmem,
+        scratch_shapes=[
+            pltpu.VMEM((width, unit), bf16),
+            pltpu.VMEM((unit, width), bf16),
+            pltpu.VMEM((width, shared_unit), bf16),
+            pltpu.VMEM((shared_unit, width), bf16),
+            pltpu.VMEM((8 * rows, width), bf16),
+            pltpu.VMEM((8 * rows, width), bf16),
+            pltpu.VMEM((7 * rows, width), bf16),
+            pltpu.VMEM((2 * rows, unit), bf16),
+            pltpu.VMEM((rows, width), bf16),
+            pltpu.VMEM((4 * tok_dev, width), bf16),
+            pltpu.VMEM((2 * tok_dev, shared_unit), bf16),
+            pltpu.VMEM((4 * tok_dev, width), bf16),
+            pltpu.VMEM((tok_dev, width), bf16),
+            pltpu.VMEM((tok_dev, width), bf16),
+            pltpu.VMEM((tok_dev, width), bf16),
+            pltpu.VMEM((tok_dev, width), f32),
+            dma((4,)),
+            dma,
+            dma((4,)),
+            dma((4,)),
+            dma((2, 4, 4)),
+            dma((2, 5, 4)),
+            dma((2, 4, 4)),
+            dma((2, 4, 4)),
+            dma((4,)),
+            dma((4,)),
+            dma((3, 2)),
+            dma((3, 2)),
+            dma((3, 4)),
+            dma((3, 4)),
+        ],
+        compiler_params=pltpu.CompilerParams(
+            collective_id=0, has_side_effects=True, vmem_limit_bytes=62 * 1024 * 1024
+        ),
+    )(
+        outgoing,
+        back_map,
+        residual + group_bias,
+        group_b1,
+        shared_gain[None, :],
+        shared_b1[None, :],
+        shared_b2[None, :],
+        group_w1[0],
+        group_w2[0],
+        shared_w1,
+        shared_w2,
+    )
+
+
+def plain_on_device(
     tokens,
     languages,
     lang_group,
@@ -120,8 +627,9 @@
         P("group", None),
         P(),
     )
+    fits = mesh.shape["group"] == 4 and mesh.shape["within"] == 8
     return jax.shard_map(
-        on_device,
+        fused_on_device if fits else plain_on_device,
         mesh=mesh,
         in_specs=placed,
         out_specs=P(("group", "within"), None),

time: 360 us -> 178 us (0.49)
  waiting for transfers between devices: 268 us -> 0 us
  Pallas kernels: 0 us -> 165 us
  matrix products: 39.8 us -> 5.67 us
  blocking collectives: 30.9 us -> 0 us
  between operations: 13.2 us -> 0.03 us
    pallas_call x0 -> x1, Pallas kernels: none -> 165 us  [fused_on_device(): pl.pallas_call(functools.partial(fused_kernel, cap), out_shape=jax.ShapeD...]
    reduce_scatter x2 -> x0, waiting for transfers between devices: 148 us -> none  [the longest x1 116 us: on_device(): lax.psum_scatter(jnp.dot(selected, second_proj, preferred_element_type=jn...]
    all_gather x2 -> x0, waiting for transfers between devices: 121 us -> none  [the longest x1 99.8 us: on_device(): lax.all_gather(group_rows, 'within', axis=0, tiled=True)]
    dot_general x6 -> x3, matrix products: 39.8 us -> 5.67 us  [the longest x1 2.68 us: fused_on_device(): jnp.dot(onehot_float, group_b2, precision=lax.Precision.HIGHEST)]
    all_to_all x2 -> x0, blocking collectives: 30.9 us -> none  [the longest x1 15.8 us: on_device(): lax.all_to_all(outgoing, 'group', split_axis=0, concat_axis=0, tiled=True)]
  transfers between devices with their start and end apart: 4 -> 0, of which waited for: 4 -> 0; matrix products, arithmetic and copies ran while one was open for 0% -> 0% of each run, Pallas kernels for 0% -> 0%
where the time goes in v1:
time: 178 us; the launch traced here: 177 us
  Pallas kernels  165 us (93%)
  matrix products  5.67 us (3%)
  other arithmetic  4.22 us (2%)
  local copies, waits for them, and re-layouts  1.89 us (1%)
    pallas_call x1, Pallas kernels, fused_on_device(): pl.pallas_call(functools.partial(fused_kernel, cap), out_shape=jax.ShapeD...  165 us

profile of v1, /device:TPU:0, one launch (start us, length us, event | category | flops | bytes accessed | tf_op | source)
XLA Modules:
  0.0 177.2 jit_solution(229108698663328399)
XLA Ops:
  0.0 0.0 copy-start
  0.0 0.8 select_reduce_fusion
  0.8 0.2 convert_reduce_fusion.1
  1.0 1.2 convert_reduce_fusion
  2.2 1.3 fusion.3
  3.5 0.7 fusion.4.back_map
  4.2 0.0 copy-done
  4.2 1.7 fusion
  6.0 1.3 convolution_convert_fusion.out_rows
  7.2 2.7 %convolution_add_fusion.residual = f32[128,2048]{1,0:T(8,128)} fusion(f32[4,2048]{1,0:T(4,128)} %param.20, bf16[128,2048]{1,0:T(8,128)(2,1)} %param.13, s32[128]{0:T(128)S(1)} %select_reduce_fusion), kind=kOutput, calls=%fused_computation.1 | convolution fusion | flops 13107712 | bytes 1606144 | tf_op jit(solution)/shard_map/dot_general | solution.py:458
  9.9 165.3 %shard_map.127 = bf16[128,2048]{1,0:T(8,128)(2,1)} custom-call(bf16[192,2048]{1,0:T(8,128)(2,1)} %convolution_convert_fusion.out_rows, bf16[128,192]{1,0:T(8,128)(2,1)} %fusion.4.back_map, f32[128,2048]{1,0:T(8,128)} %convolution_add_fusion.residual, f32[1,1024]{1,0:T(1,128)} %b1.1, f32[1,2048]{1,0:T(1,128)} %bitcast.10, f32[1,2048]{1,0:T(1,128)} %bitcast.11, ...), custom_call_target="tpu_custom_call" | custom-call | tf_op jit(solution)/shard_map/pallas_call | solution.py:466
  175.3 1.9 %copy.15 = bf16[128,2048]{1,0:T(8,128)(2,1)} copy(bf16[128,2048]{1,0:T(8,128)(2,1)} %shard_map.127) | data formatting | bytes 1048576
  (3 shorter events, 0.0 us)
Async XLA Ops:
  0.0 4.2 %copy-start = (f32[4,2048]{1,0:T(4,128)S(1)}, f32[4,2048]{1,0:T(4,128)}, u32[]{:S(2)}) copy-start(f32[4,2048]{1,0:T(4,128)} %param.16) | copy-start | bytes 98308

commit v2 on v0

--- a/solution.py
+++ b/solution.py
@@ -1,7 +1,12 @@
 import jax
 import jax.numpy as jnp
 from jax import lax
+from jax.experimental import pallas as pl
+from jax.experimental.pallas import tpu as pltpu
 from jax.sharding import PartitionSpec as P
+
+MESH = pl.DeviceIdType.MESH
+TILE = 256
 
 
 def layer_norm(values, gains):
@@ -11,7 +16,743 @@
     return centred * lax.rsqrt(spread + 1e-05) * gains
 
 
-def on_device(
+def columns(tile, size):
+    return pl.ds(pl.multiple_of(tile * size, size), size)
+
+
+def row_sum(mask):
+    return jnp.sum(jnp.where(mask, 1.0, 0.0), axis=1, keepdims=True)
+
+
+def column_sum(mask):
+    return jnp.sum(jnp.where(mask, 1.0, 0.0), axis=0, keepdims=True)
+
+
+def by_group(column, table):
+    value = jnp.where(column == 0.0, table[0:1, :], 0.0)
+    for i in range(1, table.shape[0]):
+        value = jnp.where(column == float(i), table[i : i + 1, :], value)
+    return value
+
+
+def fused_kernel(
+    tokens,
+    languages,
+    lang_group,
+    group_gain,
+    group_b2,
+    b1,
+    gain2,
+    sb1,
+    sb2,
+    w1_hbm,
+    w2_hbm,
+    sw1_hbm,
+    sw2_hbm,
+    encoded,
+    w1,
+    w2,
+    sw1,
+    sw2,
+    outgoing,
+    rows_a,
+    part_a,
+    rs_a,
+    ret_a,
+    rows_b,
+    part_b,
+    rs_b,
+    ret_b,
+    hidden,
+    sgather,
+    shidden,
+    spart,
+    sown,
+    scross,
+    ssum,
+    middle,
+    sgather_b,
+    shidden_b,
+    spart_b,
+    sown_b,
+    scross_b,
+    ssum_b,
+    middle_b,
+    back_a,
+    back_b,
+    compact,
+    spread,
+    w_sem,
+    local_sem,
+    disp_send,
+    disp_recv,
+    g_send,
+    g_recv,
+    r_send,
+    r_recv,
+    ret_send,
+    ret_recv,
+    sg_send,
+    sg_recv,
+    sr_send,
+    sr_recv,
+):
+    bf16, f32 = jnp.bfloat16, jnp.float32
+    g = lax.axis_index("group")
+    w = lax.axis_index("within")
+    x, z = lax.rem(w, 2), lax.div(w, 2)
+    p = z + x * (7 - 2 * z)
+
+    def device_at(q):
+        q = lax.rem(q + 8, 8)
+        far = lax.div(q, 4)
+        return 2 * q + far * (15 - 4 * q)
+
+    right = (g, device_at(p + 1))
+    left = (g, device_at(p - 1))
+    yy, core = lax.div(g, 2), lax.rem(g, 2)
+    peers = [
+        None,
+        (2 * yy + 1 - core, w),
+        (2 * (1 - yy) + core, w),
+        (2 * (1 - yy) + 1 - core, w),
+    ]
+    barrier = pltpu.get_barrier_semaphore()
+    for device in (right, left, peers[1], peers[2], peers[3]):
+        pl.semaphore_signal(barrier, inc=1, device_id=device, device_id_type=MESH)
+
+    loads = []
+    for i, (src, dst) in enumerate(
+        ((w1_hbm, w1), (w2_hbm, w2), (sw1_hbm, sw1), (sw2_hbm, sw2))
+    ):
+        copy = pltpu.make_async_copy(src, dst, w_sem.at[i])
+        copy.start()
+        loads.append(copy)
+
+    count = tokens.shape[0]
+    cap_a, cap_b = count // 4, count // 8
+    late = count // 4
+    i0 = lax.broadcasted_iota(jnp.int32, (count, count), 0)
+    i1 = lax.broadcasted_iota(jnp.int32, (count, count), 1)
+    eye = i0 == i1
+
+    def to_column(row):
+        return jnp.sum(jnp.where(eye, row, 0.0), axis=1, keepdims=True)
+
+    def to_row(column):
+        return jnp.sum(jnp.where(eye, column, 0.0), axis=0, keepdims=True)
+
+    num_langs = lang_group.shape[1]
+    lang = to_column(languages[...].astype(f32))
+    lang_ids = lax.broadcasted_iota(jnp.int32, (count, num_langs), 1).astype(f32)
+    group_column = jnp.sum(
+        jnp.where(lang == lang_ids, lang_group[...].astype(f32), 0.0), axis=1, keepdims=True
+    )
+    group_row = to_row(group_column)
+    same = group_column == group_row
+    slot_column = row_sum(same & (i1 < i0))
+    slot_row = column_sum(same & (i0 < i1))
+    my_y, my_core = yy.astype(f32), core.astype(f32)
+
+    def position(group, slot):
+        gy = jnp.where(group >= 2.0, 1.0, 0.0)
+        dy, dc = gy - my_y, group - 2.0 * gy - my_core
+        r = 2.0 * dy * dy + dc * dc
+        return jnp.where(
+            slot < cap_a, r * cap_a + slot, count + r * cap_b + slot - cap_a
+        )
+
+    place_column = position(group_column, slot_column)
+    place_row = position(group_row, slot_row)
+    total_slots = 4 * (cap_a + cap_b)
+    out_map = (
+        lax.broadcasted_iota(jnp.int32, (total_slots, count), 0).astype(f32) == place_row
+    )
+    normed = layer_norm(
+        tokens[...].astype(f32), by_group(group_column, group_gain)
+    ).astype(bf16)
+    outgoing[...] = jnp.dot(
+        jnp.where(out_map, 1.0, 0.0).astype(bf16), normed, preferred_element_type=f32
+    ).astype(bf16)
+    base = {"a": 0, "b": 4 * cap_a}
+    caps = {"a": cap_a, "b": cap_b}
+    stage = {"a": 0, "b": 1}
+    rows = {"a": rows_a, "b": rows_b}
+    part = {"a": part_a, "b": part_b}
+    rs = {"a": rs_a, "b": rs_b}
+    ret = {"a": ret_a, "b": ret_b}
+    own = {}
+    for k in "ab":
+        own[k] = pltpu.make_async_copy(
+            outgoing.at[pl.ds(base[k], caps[k])],
+            rows[k].at[pl.ds(0, caps[k])],
+            local_sem.at[stage[k]],
+        )
+        own[k].start()
+    pl.semaphore_wait(barrier, 5)
+
+    pending = []
+
+    def send(src, dst, send_sem, recv_sem, device):
+        copy = pltpu.make_async_remote_copy(
+            src_ref=src,
+            dst_ref=dst,
+            send_sem=send_sem,
+            recv_sem=recv_sem,
+            device_id=device,
+            device_id_type=MESH,
+        )
+        copy.start()
+        pending.append(copy)
+        return copy
+
+    def chunk(k, slot, c):
+        return pl.ds((slot * 4 + c) * caps[k], caps[k])
+
+    dispatch = {}
+    for k in "ab":
+        for r in (2, 3, 1):
+            dispatch[k, r] = send(
+                outgoing.at[pl.ds(base[k] + r * caps[k], caps[k])],
+                rows[k].at[chunk(k, 0, r)],
+                disp_send.at[stage[k], r],
+                disp_recv.at[stage[k], r],
+                peers[r],
+            )
+
+    def slot_of(way, s):
+        return 7 if s == 4 else (0 if s == 0 else 2 * s - 1 + way)
+
+    arrivals = {}
+
+    def forward(k, way, s, c):
+        arrivals[k, way, s + 1, c] = send(
+            rows[k].at[chunk(k, slot_of(way, s), c)],
+            rows[k].at[chunk(k, slot_of(way, s + 1), c)],
+            g_send.at[stage[k], way, s, c],
+            g_recv.at[stage[k], way, s + 1, c],
+            right if way == 0 else left,
+        )
+
+    def first_tiles(k, slot, slots, begin, end):
+        size = slots * 4 * caps[k]
+
+        def body(i, carry):
+            cols = columns(i, TILE)
+            value = jnp.dot(
+                rows[k][pl.ds(slot * 4 * caps[k], size), :],
+                w1[:, cols],
+                preferred_element_type=f32,
+            )
+            hidden[pl.ds(0, size), cols] = jnp.maximum(value + b1[:, cols], 0.0).astype(bf16)
+            return carry
+
+        lax.fori_loop(begin, end, body, 0)
+
+    def second_tiles(k, slot, slots, begin, end):
+        size = slots * 4 * caps[k]
+
+        def body(i, carry):
+            cols = columns(i, TILE)
+            part[k][pl.ds(slot * 4 * caps[k], size), cols] = jnp.dot(
+                hidden[pl.ds(0, size), :], w2[:, cols], preferred_element_type=f32
+            ).astype(bf16)
+            return carry
+
+        lax.fori_loop(begin, end, body, 0)
+
+    n1, n2 = w1.shape[1] // TILE, w2.shape[1] // TILE
+
+    def piece(k, slot, slots, c):
+        if c < 2:
+            first_tiles(k, slot, slots, c * n1 // 2, (c + 1) * n1 // 2)
+        else:
+            second_tiles(k, slot, slots, (c - 2) * n2 // 2, (c - 1) * n2 // 2)
+
+    def whole(k, slot, slots):
+        first_tiles(k, slot, slots, 0, n1)
+        second_tiles(k, slot, slots, 0, n2)
+
+    def gather_start(k):
+        own[k].wait()
+        for c in range(4):
+            if c:
+                dispatch[k, c].wait_recv()
+            forward(k, 0, 0, c)
+            forward(k, 1, 0, c)
+
+    def gather_step(k, s, c):
+        for way in (0, 1):
+            arrivals[k, way, s, c].wait_recv()
+            if s < 3 or c // 2 == way:
+                forward(k, way, s, c)
+
+    def rs_slot(way, t):
+        return (7, 6 - way, 4 - way, 2 - way)[t]
+
+    def rs_chunk(k, way, t, c):
+        at = way * 14 + (c % 2 if t == 0 else 4 * t - 2 + c)
+        return pl.ds(at * caps[k], caps[k])
+
+    sums = {}
+
+    def pass_on(k, way, t, c):
+        sums[k, way, t, c] = send(
+            part[k].at[chunk(k, rs_slot(way, t), c)],
+            rs[k].at[rs_chunk(k, way, t, c)],
+            r_send.at[stage[k], way, t, c],
+            r_recv.at[stage[k], way, t, c],
+            right if way == 0 else left,
+        )
+
+    def add_in(k, way, t, c):
+        sums[k, way, t, c].wait_recv()
+        here = chunk(k, rs_slot(way, t + 1), c)
+        part[k][here, :] = (
+            part[k][here, :].astype(f32) + rs[k][rs_chunk(k, way, t, c), :].astype(f32)
+        ).astype(bf16)
+        pass_on(k, way, t + 1, c)
+
+    order = (2, 3, 0, 1)
+
+    def reduce_start(k, between):
+        for c in (2, 3):
+            pass_on(k, 0, 1, c)
+            pass_on(k, 1, 1, c - 2)
+        between()
+        for c in (0, 1):
+            arrivals[k, 0, 4, c].wait_recv()
+            arrivals[k, 1, 4, c + 2].wait_recv()
+        whole(k, 7, 1)
+        for c in (0, 1):
+            pass_on(k, 0, 0, c)
+            pass_on(k, 1, 0, c + 2)
+        between()
+        for c in (0, 1):
+            add_in(k, 0, 0, c)
+            add_in(k, 1, 0, c + 2)
+
+    returned = {}
+
+    def reduce_end(k, c):
+        sums[k, 0, 3, c].wait_recv()
+        sums[k, 1, 3, c].wait_recv()
+        here = chunk(k, 0, c)
+        total = (
+            part[k][here, :].astype(f32)
+            + rs[k][rs_chunk(k, 0, 3, c), :].astype(f32)
+            + rs[k][rs_chunk(k, 1, 3, c), :].astype(f32)
+        ).astype(bf16)
+        if c == 0:
+            ret[k][pl.ds(0, caps[k]), :] = total
+        else:
+            part[k][here, :] = total
+            returned[k, c] = send(
+                part[k].at[here],
+                ret[k].at[pl.ds(c * caps[k], caps[k])],
+                ret_send.at[stage[k], c],
+                ret_recv.at[stage[k], c],
+                peers[c],
+            )
+
+    m1, m2 = sw1.shape[1] // TILE, sw2.shape[1] // TILE
+
+    def shared_first(source, start, size, target, begin, end):
+        def body(i, carry):
+            cols = columns(i, TILE)
+            value = jnp.dot(
+                source[pl.ds(start, size), :], sw1[:, cols], preferred_element_type=f32
+            )
+            target[:, cols] = jnp.maximum(value + sb1[:, cols], 0.0).astype(bf16)
+            return carry
+
+        lax.fori_loop(begin, end, body, 0)
+
+    def shared_second(source, target, start, size, begin, end):
+        def body(i, carry):
+            cols = columns(i, TILE)
+            target[pl.ds(start, size), cols] = jnp.dot(
+                source[...], sw2[:, cols], preferred_element_type=f32
+            ).astype(bf16)
+            return carry
+
+        lax.fori_loop(begin, end, body, 0)
+
+    quarters = 4
+    width = sw2.shape[1] // quarters
+
+    def quarter(q):
+        return pl.ds(q * width, width)
+
+    def add_crossed(source, cross, target, at, copy, send_sem, recv_sem, q):
+        cols = quarter(q)
+        copy.wait_recv()
+        source[at, cols] = (
+            source[at, cols].astype(f32) + cross[:, cols].astype(f32)
+        ).astype(bf16)
+        return send(source.at[at, cols], target.at[:, cols], send_sem, recv_sem, peers[2])
+
+    def combined(total, own_part, sibling, crossed, cols):
+        return (
+            total
+            + (own_part.astype(f32) + sibling.astype(f32) + crossed.astype(f32))
+            + sb2[:, cols]
+        )
+
+    half = count // 2
+
+    def block(r, h=None):
+        if h is None:
+            return pl.ds(r * count, count)
+        return pl.ds(r * count + h * half, half)
+
+    def shared_a():
+        for c in (1, 2, 3):
+            returned["a", c].wait_recv()
+        from_sibling, from_y, from_far = [], [], []
+        for h in range(2):
+            some = pl.ds(h * half, half)
+            value = middle[some, :] + jnp.dot(
+                back_a[some, :], ret_a[...], preferred_element_type=f32
+            )
+            middle[some, :] = value
+            sgather[some, :] = layer_norm(value, gain2[...]).astype(bf16)
+            for r, into in ((2, from_y), (1, from_sibling)):
+                into.append(
+                    send(
+                        sgather.at[some],
+                        sgather.at[block(r, h)],
+                        sg_send.at[r, h],
+                        sg_recv.at[r, h],
+                        peers[r],
+                    )
+                )
+        yield
+        loads[2].wait()
+        loads[3].wait()
+        for h in range(2):
+            from_sibling[h].wait_recv()
+        for q in range(4):
+            shared_first(sgather, 0, 2 * count, shidden, q * m1 // 4, (q + 1) * m1 // 4)
+            yield
+        for q in range(4):
+            shared_second(shidden, spart, 0, 2 * count, q * m2 // 4, (q + 1) * m2 // 4)
+            yield
+        to_own = send(
+            spart.at[block(1)], sown, sr_send.at[2, 0], sr_recv.at[2, 0], peers[1]
+        )
+        yield
+        for h in range(2):
+            from_y[h].wait_recv()
+            from_far.append(
+                send(
+                    sgather.at[block(2, h)],
+                    sgather.at[block(3, h)],
+                    sg_send.at[3, h],
+                    sg_recv.at[3, h],
+                    peers[1],
+                )
+            )
+            yield
+        for h in range(2):
+            from_far[h].wait_recv()
+        for q in range(4):
+            shared_first(
+                sgather, 2 * count, 2 * count, shidden, q * m1 // 4, (q + 1) * m1 // 4
+            )
+            yield
+        crossed, summed = [], []
+
+        def finish(q):
+            summed.append(
+                add_crossed(
+                    spart, scross, ssum, block(2), crossed[q], sr_send.at[1, q], sr_recv.at[1, q], q
+                )
+            )
+
+        for q in range(quarters):
+            shared_second(
+                shidden, spart, 2 * count, 2 * count, q * m2 // 4, (q + 1) * m2 // 4
+            )
+            crossed.append(
+                send(
+                    spart.at[block(3), quarter(q)],
+                    scross.at[:, quarter(q)],
+                    sr_send.at[0, q],
+                    sr_recv.at[0, q],
+                    peers[1],
+                )
+            )
+            if q:
+                finish(q - 1)
+            yield
+        finish(quarters - 1)
+        yield
+        to_own.wait_recv()
+        for q in range(quarters):
+            cols = quarter(q)
+            summed[q].wait_recv()
+            middle[:, cols] = combined(
+                middle[:, cols], spart[block(0), cols], sown[:, cols], ssum[:, cols], cols
+            )
+            yield
+
+    gather_start("a")
+    back_a[...] = jnp.where(
+        lax.broadcasted_iota(jnp.int32, (count, 4 * cap_a), 1).astype(f32) == place_column,
+        1.0,
+        0.0,
+    ).astype(bf16)
+    middle[...] = tokens[...].astype(f32) + by_group(group_column, group_b2)
+    rank_row = column_sum((slot_column >= cap_a) & (i0 < i1))
+    rank_row = jnp.where(slot_row >= cap_a, rank_row, -1.0)
+    rank_column = row_sum((slot_row >= cap_a) & (i1 < i0))
+    rank_column = jnp.where(slot_column >= cap_a, rank_column, -1.0)
+    pick = jnp.where(
+        lax.broadcasted_iota(jnp.int32, (late, count), 0).astype(f32) == rank_row, 1.0, 0.0
+    )
+    compact[...] = pick.astype(bf16)
+    spread[...] = jnp.where(
+        lax.broadcasted_iota(jnp.int32, (count, late), 1).astype(f32) == rank_column, 1.0, 0.0
+    ).astype(bf16)
+    late_place = jnp.sum(pick * place_row, axis=1, keepdims=True) - 4.0 * cap_a
+    late_group = jnp.sum(pick * group_row, axis=1, keepdims=True)
+    back_b[...] = jnp.where(
+        lax.broadcasted_iota(jnp.int32, (late, 4 * cap_b), 1).astype(f32) == late_place,
+        1.0,
+        0.0,
+    ).astype(bf16)
+    middle_b[...] = jnp.dot(
+        compact[...], tokens[...], preferred_element_type=f32
+    ) + by_group(late_group, group_b2)
+    loads[0].wait()
+    loads[1].wait()
+    for s in (1, 2, 3):
+        for c in range(4):
+            gather_step("a", s, c)
+            if s == 1:
+                piece("a", 0, 1, c)
+            else:
+                piece("a", 2 * s - 3, 2, c)
+    whole("a", 5, 2)
+    reduce_start("a", lambda: None)
+    for t in (1, 2):
+        for c in order:
+            for way in (0, 1):
+                add_in("a", way, t, c)
+
+    gather_start("b")
+    for c in order:
+        reduce_end("a", c)
+    shared = shared_a()
+
+    def go_on():
+        next(shared, None)
+
+    for s in (1, 2, 3):
+        for c in range(4):
+            gather_step("b", s, c)
+            if s == 3:
+                piece("b", 0, 5, c)
+            go_on()
+    whole("b", 5, 2)
+    reduce_start("b", go_on)
+    for t in (1, 2):
+        for c in order:
+            for way in (0, 1):
+                add_in("b", way, t, c)
+            go_on()
+    for c in order:
+        reduce_end("b", c)
+        go_on()
+    for _ in shared:
+        pass
+
+    for c in (1, 2, 3):
+        returned["b", c].wait_recv()
+
+    def block_b(r):
+        return pl.ds(r * late, late)
+
+    value = middle_b[...] + jnp.dot(back_b[...], ret_b[...], preferred_element_type=f32)
+    middle_b[...] = value
+    sgather_b[block_b(0), :] = layer_norm(value, gain2[...]).astype(bf16)
+    near = {}
+    for r in (2, 1):
+        near[r] = send(
+            sgather_b.at[block_b(0)],
+            sgather_b.at[block_b(r)],
+            sg_send.at[r, 2],
+            sg_recv.at[r, 2],
+            peers[r],
+        )
+    near[2].wait_recv()
+    near[3] = send(
+        sgather_b.at[block_b(2)],
+        sgather_b.at[block_b(3)],
+        sg_send.at[3, 2],
+        sg_recv.at[3, 2],
+        peers[1],
+    )
+    near[1].wait_recv()
+    near[3].wait_recv()
+    shared_first(sgather_b, 0, 4 * late, shidden_b, 0, m1)
+    crossed, to_own, summed = [], [], []
+
+    def finish_b(q):
+        summed.append(
+            add_crossed(
+                spart_b,
+                scross_b,
+                ssum_b,
+                block_b(2),
+                crossed[q],
+                sr_send.at[4, q],
+                sr_recv.at[4, q],
+                q,
+            )
+        )
+
+    for q in range(quarters):
+        cols = quarter(q)
+        shared_second(shidden_b, spart_b, 0, 4 * late, q * m2 // 4, (q + 1) * m2 // 4)
+        crossed.append(
+            send(
+                spart_b.at[block_b(3), cols],
+                scross_b.at[:, cols],
+                sr_send.at[3, q],
+                sr_recv.at[3, q],
+                peers[1],
+            )
+        )
+        to_own.append(
+            send(
+                spart_b.at[block_b(1), cols],
+                sown_b.at[:, cols],
+                sr_send.at[5, q],
+                sr_recv.at[5, q],
+                peers[1],
+            )
+        )
+        if q:
+            finish_b(q - 1)
+    finish_b(quarters - 1)
+    for q in range(quarters):
+        cols = quarter(q)
+        to_own[q].wait_recv()
+        summed[q].wait_recv()
+        late_out = combined(
+            middle_b[:, cols], spart_b[block_b(0), cols], sown_b[:, cols], ssum_b[:, cols], cols
+        ).astype(bf16)
+        placed = jnp.dot(spread[...], late_out, preferred_element_type=f32)
+        is_late = jnp.sum(spread[...].astype(f32), axis=1, keepdims=True)
+        encoded[:, cols] = jnp.where(is_late > 0.5, placed, middle[:, cols]).astype(bf16)
+    for copy in pending:
+        copy.wait_send()
+
+
+def fused_on_device(
+    tokens,
+    languages,
+    lang_group,
+    group_gain,
+    group_w1,
+    group_b1,
+    group_w2,
+    group_b2,
+    shared_gain,
+    shared_w1,
+    shared_b1,
+    shared_w2,
+    shared_b2,
+):
+    count, width = tokens.shape
+    unit = group_w1.shape[2]
+    shared_unit = shared_w1.shape[1]
+    cap_a, cap_b = count // 4, count // 8
+    late = count // 4
+    bf16, f32 = jnp.bfloat16, jnp.float32
+    in_vmem = pl.BlockSpec(memory_space=pltpu.VMEM)
+    anywhere = pl.BlockSpec(memory_space=pl.ANY)
+    dma = pltpu.SemaphoreType.DMA
+
+    def held(rows, columns=width, dtype=bf16):
+        return pltpu.VMEM((rows, columns), dtype)
+
+    return pl.pallas_call(
+        fused_kernel,
+        out_shape=jax.ShapeDtypeStruct((count, width), bf16),
+        in_specs=[in_vmem] * 9 + [anywhere] * 4,
+        out_specs=in_vmem,
+        scratch_shapes=[
+            held(width, unit),
+            held(unit),
+            held(width, shared_unit),
+            held(shared_unit),
+            held(4 * (cap_a + cap_b)),
+            held(32 * cap_a),
+            held(32 * cap_a),
+            held(28 * cap_a),
+            held(4 * cap_a),
+            held(32 * cap_b),
+            held(32 * cap_b),
+            held(28 * cap_b),
+            held(4 * cap_b),
+            held(max(8 * cap_a, 20 * cap_b), unit),
+            held(4 * count),
+            held(2 * count, shared_unit),
+            held(4 * count),
+            held(count),
+            held(count),
+            held(count),
+            held(count, dtype=f32),
+            held(4 * late),
+            held(4 * late, shared_unit),
+            held(4 * late),
+            held(late),
+            held(late),
+            held(late),
+            held(late, dtype=f32),
+            held(count, 4 * cap_a),
+            held(late, 4 * cap_b),
+            held(late, count),
+            held(count, late),
+            dma((4,)),
+            dma((2,)),
+            dma((2, 4)),
+            dma((2, 4)),
+            dma((2, 2, 4, 4)),
+            dma((2, 2, 5, 4)),
+            dma((2, 2, 4, 4)),
+            dma((2, 2, 4, 4)),
+            dma((2, 4)),
+            dma((2, 4)),
+            dma((4, 3)),
+            dma((4, 3)),
+            dma((6, 4)),
+            dma((6, 4)),
+        ],
+        compiler_params=pltpu.CompilerParams(
+            collective_id=0, has_side_effects=True, vmem_limit_bytes=62 * 1024 * 1024
+        ),
+    )(
+        tokens,
+        languages[None, :],
+        lang_group[None, :],
+        group_gain,
+        group_b2,
+        group_b1,
+        shared_gain[None, :],
+        shared_b1[None, :],
+        shared_b2[None, :],
+        group_w1[0],
+        group_w2[0],
+        shared_w1,
+        shared_w2,
+    )
+
+
+def plain_on_device(
     tokens,
     languages,
     lang_group,
@@ -120,8 +861,9 @@
         P("group", None),
         P(),
     )
+    fits = mesh.shape["group"] == 4 and mesh.shape["within"] == 8
     return jax.shard_map(
-        on_device,
+        fused_on_device if fits else plain_on_device,
         mesh=mesh,
         in_specs=placed,
         out_specs=P(("group", "within"), None),

time: 360 us -> 166 us (0.46)
  waiting for transfers between devices: 268 us -> 0 us
  Pallas kernels: 0 us -> 164 us
  matrix products: 39.8 us -> 0 us
  blocking collectives: 30.9 us -> 0 us
  between operations: 13.2 us -> 0.01 us
  other arithmetic: 7.03 us -> 0 us
    pallas_call x0 -> x1, Pallas kernels: none -> 164 us  [fused_on_device(): pl.pallas_call(fused_kernel, out_shape=jax.ShapeDtypeStruct((count, width...]
    reduce_scatter x2 -> x0, waiting for transfers between devices: 148 us -> none  [the longest x1 116 us: on_device(): lax.psum_scatter(jnp.dot(selected, second_proj, preferred_element_type=jn...]
    all_gather x2 -> x0, waiting for transfers between devices: 121 us -> none  [the longest x1 99.8 us: on_device(): lax.all_gather(group_rows, 'within', axis=0, tiled=True)]
    dot_general x6 -> x0, matrix products: 39.8 us -> none  [the longest x1 19.3 us: on_device(): jnp.dot(selected, second_proj, preferred_element_type=jnp.float32)]
    all_to_all x2 -> x0, blocking collectives: 30.9 us -> none  [the longest x1 15.8 us: on_device(): lax.all_to_all(outgoing, 'group', split_axis=0, concat_axis=0, tiled=True)]
    reduce_sum x5 -> x0, other arithmetic: 3.74 us -> none  [the longest x2 1.59 us: layer_norm(): spread = jnp.mean(centred * centred, axis=-1, keepdims=True)]
  transfers between devices with their start and end apart: 4 -> 0, of which waited for: 4 -> 0; matrix products, arithmetic and copies ran while one was open for 0% -> 0% of each run, Pallas kernels for 0% -> 0%
where the time goes in v2:
time: 166 us
  Pallas kernels  164 us (99%)
  local copies, waits for them, and re-layouts  1.88 us (1%)
    pallas_call x1, Pallas kernels, fused_on_device(): pl.pallas_call(fused_kernel, out_shape=jax.ShapeDtypeStruct((count, width...  164 us

profile of v2, /device:TPU:0, one launch (start us, length us, event | category | flops | bytes accessed | tf_op | source)
XLA Modules:
  0.0 165.8 jit_solution(15091178923290552927)
XLA Ops:
  0.0 163.9 %shard_map.127 = bf16[128,2048]{1,0:T(8,128)(2,1)} custom-call(bf16[128,2048]{1,0:T(8,128)(2,1)} %tokens.1, s32[1,128]{1,0:T(1,128)} %bitcast.12, s32[1,100]{1,0:T(1,128)} %bitcast.13, f32[4,2048]{1,0:T(4,128)} %group_gain.1, f32[4,2048]{1,0:T(4,128)} %group_b2.1, f32[1,1024]{1,0:T(1,128)} %b1.1, f32[1,2048]{1,0:T(1,128)} %bitcast.9, f32[1,2048]{1,0:T(1,128)} %bitcast.10, ...), custom_call_target="tpu_custom_call" | custom-call | tf_op jit(solution)/shard_map/pallas_call | solution.py:682
  163.9 1.9 %copy.15 = bf16[128,2048]{1,0:T(8,128)(2,1)} copy(bf16[128,2048]{1,0:T(8,128)(2,1)} %shard_map.127) | data formatting | bytes 1048576

commit v3 on v2

--- a/solution.py
+++ b/solution.py
@@ -206,6 +206,10 @@
         pending.append(copy)
         return copy
 
+    def drain(keep):
+        while len(pending) > keep:
+            pending.pop(0).wait_send()
+
     def chunk(k, slot, c):
         return pl.ds((slot * 4 + c) * caps[k], caps[k])
 
@@ -534,27 +538,28 @@
                 piece("a", 0, 1, c)
             else:
                 piece("a", 2 * s - 3, 2, c)
+    gather_start("b")
     whole("a", 5, 2)
     reduce_start("a", lambda: None)
+    drain(16)
     for t in (1, 2):
-        for c in order:
+        for c in range(4):
             for way in (0, 1):
-                add_in("a", way, t, c)
-
-    gather_start("b")
-    for c in order:
-        reduce_end("a", c)
+                add_in("a", way, t, order[c])
+            gather_step("b", t, c)
+        if t == 1:
+            drain(32)
+    for c in range(4):
+        reduce_end("a", order[c])
+        gather_step("b", 3, c)
+        piece("b", 0, 5, c)
+
     shared = shared_a()
 
     def go_on():
         next(shared, None)
 
-    for s in (1, 2, 3):
-        for c in range(4):
-            gather_step("b", s, c)
-            if s == 3:
-                piece("b", 0, 5, c)
-            go_on()
+    go_on()
     whole("b", 5, 2)
     reduce_start("b", go_on)
     for t in (1, 2):
@@ -565,8 +570,8 @@
     for c in order:
         reduce_end("b", c)
         go_on()
-    for _ in shared:
-        pass
+    for _ in range(3):
+        go_on()
 
     for c in (1, 2, 3):
         returned["b", c].wait_recv()
@@ -586,6 +591,9 @@
             sg_recv.at[r, 2],
             peers[r],
         )
+    for _ in shared:
+        pass
+    drain(16)
     near[2].wait_recv()
     near[3] = send(
         sgather_b.at[block_b(2)],
@@ -647,8 +655,7 @@
         placed = jnp.dot(spread[...], late_out, preferred_element_type=f32)
         is_late = jnp.sum(spread[...].astype(f32), axis=1, keepdims=True)
         encoded[:, cols] = jnp.where(is_late > 0.5, placed, middle[:, cols]).astype(bf16)
-    for copy in pending:
-        copy.wait_send()
+    drain(0)
 
 
 def fused_on_device(

time: 166 us -> 171 us (1.030)
  Pallas kernels: 164 us -> 169 us
    pallas_call x1, Pallas kernels: 164 us -> 169 us  [fused_on_device(): pl.pallas_call(fused_kernel, out_shape=jax.ShapeDtypeStruct((count, width...]
where the time goes in v3:
time: 171 us
  Pallas kernels  169 us (99%)
  local copies, waits for them, and re-layouts  1.88 us (1%)
    pallas_call x1, Pallas kernels, fused_on_device(): pl.pallas_call(fused_kernel, out_shape=jax.ShapeDtypeStruct((count, width...  169 us

profile of v3, /device:TPU:0, one launch (start us, length us, event | category | flops | bytes accessed | tf_op | source)
XLA Modules:
  0.0 171.2 jit_solution(12138788866231197283)
XLA Ops:
  0.0 169.3 %shard_map.127 = bf16[128,2048]{1,0:T(8,128)(2,1)} custom-call(bf16[128,2048]{1,0:T(8,128)(2,1)} %tokens.1, s32[1,128]{1,0:T(1,128)} %bitcast.12, s32[1,100]{1,0:T(1,128)} %bitcast.13, f32[4,2048]{1,0:T(4,128)} %group_gain.1, f32[4,2048]{1,0:T(4,128)} %group_b2.1, f32[1,1024]{1,0:T(1,128)} %b1.1, f32[1,2048]{1,0:T(1,128)} %bitcast.9, f32[1,2048]{1,0:T(1,128)} %bitcast.10, ...), custom_call_target="tpu_custom_call" | custom-call | tf_op jit(solution)/shard_map/pallas_call | solution.py:689
  169.3 1.9 %copy.15 = bf16[128,2048]{1,0:T(8,128)(2,1)} copy(bf16[128,2048]{1,0:T(8,128)(2,1)} %shard_map.127) | data formatting | bytes 1048576

commit v4 on v3

--- a/solution.py
+++ b/solution.py
@@ -6,7 +6,7 @@
 from jax.sharding import PartitionSpec as P
 
 MESH = pl.DeviceIdType.MESH
-TILE = 256
+TILE = 512
 
 
 def layer_norm(values, gains):
@@ -546,20 +546,24 @@
         for c in range(4):
             for way in (0, 1):
                 add_in("a", way, t, order[c])
-            gather_step("b", t, c)
+            if t == 2:
+                gather_step("b", 1, c)
         if t == 1:
             drain(32)
-    for c in range(4):
-        reduce_end("a", order[c])
-        gather_step("b", 3, c)
-        piece("b", 0, 5, c)
+    for c in order:
+        reduce_end("a", c)
 
     shared = shared_a()
 
     def go_on():
         next(shared, None)
 
-    go_on()
+    for s in (2, 3):
+        for c in range(4):
+            gather_step("b", s, c)
+            go_on()
+            if s == 3:
+                piece("b", 0, 5, c)
     whole("b", 5, 2)
     reduce_start("b", go_on)
     for t in (1, 2):

time: 171 us -> 166 us (0.971)
  Pallas kernels: 169 us -> 164 us
    pallas_call x1, Pallas kernels: 169 us -> 164 us  [fused_on_device(): pl.pallas_call(fused_kernel, out_shape=jax.ShapeDtypeStruct((count, width...]
where the time goes in v4:
time: 166 us
  Pallas kernels  164 us (99%)
  local copies, waits for them, and re-layouts  1.88 us (1%)
    pallas_call x1, Pallas kernels, fused_on_device(): pl.pallas_call(fused_kernel, out_shape=jax.ShapeDtypeStruct((count, width...  164 us

profile of v4, /device:TPU:0, one launch (start us, length us, event | category | flops | bytes accessed | tf_op | source)
XLA Modules:
  0.0 166.2 jit_solution(17370883373381527784)
XLA Ops:
  0.0 164.4 %shard_map.127 = bf16[128,2048]{1,0:T(8,128)(2,1)} custom-call(bf16[128,2048]{1,0:T(8,128)(2,1)} %tokens.1, s32[1,128]{1,0:T(1,128)} %bitcast.12, s32[1,100]{1,0:T(1,128)} %bitcast.13, f32[4,2048]{1,0:T(4,128)} %group_gain.1, f32[4,2048]{1,0:T(4,128)} %group_b2.1, f32[1,1024]{1,0:T(1,128)} %b1.1, f32[1,2048]{1,0:T(1,128)} %bitcast.9, f32[1,2048]{1,0:T(1,128)} %bitcast.10, ...), custom_call_target="tpu_custom_call" | custom-call | tf_op jit(solution)/shard_map/pallas_call | solution.py:693
  164.4 1.9 %copy.15 = bf16[128,2048]{1,0:T(8,128)(2,1)} copy(bf16[128,2048]{1,0:T(8,128)(2,1)} %shard_map.127) | data formatting | bytes 1048576

commit v5 on v2

--- a/solution.py
+++ b/solution.py
@@ -6,7 +6,7 @@
 from jax.sharding import PartitionSpec as P
 
 MESH = pl.DeviceIdType.MESH
-TILE = 256
+TILE = 512
 
 
 def layer_norm(values, gains):
@@ -206,15 +206,19 @@
         pending.append(copy)
         return copy
 
+    def drain(keep):
+        while len(pending) > keep:
+            pending.pop(0).wait_send()
+
     def chunk(k, slot, c):
-        return pl.ds((slot * 4 + c) * caps[k], caps[k])
+        return pl.ds((slot * 4 + 2 * c) * caps[k], 2 * caps[k])
 
     dispatch = {}
     for k in "ab":
         for r in (2, 3, 1):
             dispatch[k, r] = send(
                 outgoing.at[pl.ds(base[k] + r * caps[k], caps[k])],
-                rows[k].at[chunk(k, 0, r)],
+                rows[k].at[pl.ds(r * caps[k], caps[k])],
                 disp_send.at[stage[k], r],
                 disp_recv.at[stage[k], r],
                 peers[r],
@@ -275,24 +279,25 @@
 
     def gather_start(k):
         own[k].wait()
-        for c in range(4):
-            if c:
-                dispatch[k, c].wait_recv()
+        for c in range(2):
+            for r in (2 * c, 2 * c + 1):
+                if r:
+                    dispatch[k, r].wait_recv()
             forward(k, 0, 0, c)
             forward(k, 1, 0, c)
 
     def gather_step(k, s, c):
         for way in (0, 1):
             arrivals[k, way, s, c].wait_recv()
-            if s < 3 or c // 2 == way:
+            if s < 3 or c == way:
                 forward(k, way, s, c)
 
     def rs_slot(way, t):
         return (7, 6 - way, 4 - way, 2 - way)[t]
 
     def rs_chunk(k, way, t, c):
-        at = way * 14 + (c % 2 if t == 0 else 4 * t - 2 + c)
-        return pl.ds(at * caps[k], caps[k])
+        at = way * 14 + (0 if t == 0 else 4 * t - 2 + 2 * c)
+        return pl.ds(at * caps[k], 2 * caps[k])
 
     sums = {}
 
@@ -313,24 +318,20 @@
         ).astype(bf16)
         pass_on(k, way, t + 1, c)
 
-    order = (2, 3, 0, 1)
+    order = (1, 0)
 
     def reduce_start(k, between):
-        for c in (2, 3):
-            pass_on(k, 0, 1, c)
-            pass_on(k, 1, 1, c - 2)
+        pass_on(k, 0, 1, 1)
+        pass_on(k, 1, 1, 0)
         between()
-        for c in (0, 1):
-            arrivals[k, 0, 4, c].wait_recv()
-            arrivals[k, 1, 4, c + 2].wait_recv()
+        arrivals[k, 0, 4, 0].wait_recv()
+        arrivals[k, 1, 4, 1].wait_recv()
         whole(k, 7, 1)
-        for c in (0, 1):
-            pass_on(k, 0, 0, c)
-            pass_on(k, 1, 0, c + 2)
+        pass_on(k, 0, 0, 0)
+        pass_on(k, 1, 0, 1)
         between()
-        for c in (0, 1):
-            add_in(k, 0, 0, c)
-            add_in(k, 1, 0, c + 2)
+        add_in(k, 0, 0, 0)
+        add_in(k, 1, 0, 1)
 
     returned = {}
 
@@ -344,16 +345,17 @@
             + rs[k][rs_chunk(k, 1, 3, c), :].astype(f32)
         ).astype(bf16)
         if c == 0:
-            ret[k][pl.ds(0, caps[k]), :] = total
-        else:
-            part[k][here, :] = total
-            returned[k, c] = send(
-                part[k].at[here],
-                ret[k].at[pl.ds(c * caps[k], caps[k])],
-                ret_send.at[stage[k], c],
-                ret_recv.at[stage[k], c],
-                peers[c],
-            )
+            ret[k][pl.ds(0, caps[k]), :] = total[: caps[k], :]
+        part[k][here, :] = total
+        for r in (2 * c, 2 * c + 1):
+            if r:
+                returned[k, r] = send(
+                    part[k].at[pl.ds(r * caps[k], caps[k])],
+                    ret[k].at[pl.ds(r * caps[k], caps[k])],
+                    ret_send.at[stage[k], r],
+                    ret_recv.at[stage[k], r],
+                    peers[r],
+                )
 
     m1, m2 = sw1.shape[1] // TILE, sw2.shape[1] // TILE
 
@@ -528,14 +530,16 @@
     loads[0].wait()
     loads[1].wait()
     for s in (1, 2, 3):
-        for c in range(4):
+        for c in range(2):
             gather_step("a", s, c)
-            if s == 1:
-                piece("a", 0, 1, c)
-            else:
-                piece("a", 2 * s - 3, 2, c)
+            for i in (2 * c, 2 * c + 1):
+                if s == 1:
+                    piece("a", 0, 1, i)
+                else:
+                    piece("a", 2 * s - 3, 2, i)
     whole("a", 5, 2)
     reduce_start("a", lambda: None)
+    drain(8)
     for t in (1, 2):
         for c in order:
             for way in (0, 1):
@@ -546,17 +550,19 @@
         reduce_end("a", c)
     shared = shared_a()
 
-    def go_on():
-        next(shared, None)
+    def go_on(pieces=2):
+        for _ in range(pieces):
+            next(shared, None)
 
     for s in (1, 2, 3):
-        for c in range(4):
+        for c in range(2):
             gather_step("b", s, c)
             if s == 3:
-                piece("b", 0, 5, c)
+                piece("b", 0, 5, 2 * c)
+                piece("b", 0, 5, 2 * c + 1)
             go_on()
     whole("b", 5, 2)
-    reduce_start("b", go_on)
+    reduce_start("b", lambda: go_on(1))
     for t in (1, 2):
         for c in order:
             for way in (0, 1):
@@ -565,8 +571,6 @@
     for c in order:
         reduce_end("b", c)
         go_on()
-    for _ in shared:
-        pass
 
     for c in (1, 2, 3):
         returned["b", c].wait_recv()
@@ -586,6 +590,9 @@
             sg_recv.at[r, 2],
             peers[r],
         )
+    for _ in shared:
+        pass
+    drain(16)
     near[2].wait_recv()
     near[3] = send(
         sgather_b.at[block_b(2)],
@@ -647,8 +654,7 @@
         placed = jnp.dot(spread[...], late_out, preferred_element_type=f32)
         is_late = jnp.sum(spread[...].astype(f32), axis=1, keepdims=True)
         encoded[:, cols] = jnp.where(is_late > 0.5, placed, middle[:, cols]).astype(bf16)
-    for copy in pending:
-        copy.wait_send()
+    drain(0)
 
 
 def fused_on_device(
@@ -721,10 +727,10 @@
             dma((2,)),
             dma((2, 4)),
             dma((2, 4)),
-            dma((2, 2, 4, 4)),
-            dma((2, 2, 5, 4)),
-            dma((2, 2, 4, 4)),
-            dma((2, 2, 4, 4)),
+            dma((2, 2, 4, 2)),
+            dma((2, 2, 5, 2)),
+            dma((2, 2, 4, 2)),
+            dma((2, 2, 4, 2)),
             dma((2, 4)),
             dma((2, 4)),
             dma((4, 3)),

time: 166 us -> 166 us (level)
  no operation moved by 1% of the time
where the time goes in v5:
time: 166 us
  Pallas kernels  164 us (99%)
  local copies, waits for them, and re-layouts  1.88 us (1%)
    pallas_call x1, Pallas kernels, fused_on_device(): pl.pallas_call(fused_kernel, out_shape=jax.ShapeDtypeStruct((count, width...  164 us

profile of v5, /device:TPU:0, one launch (start us, length us, event | category | flops | bytes accessed | tf_op | source)
XLA Modules:
  0.0 165.9 jit_solution(1788045890739723048)
XLA Ops:
  0.0 164.0 %shard_map.127 = bf16[128,2048]{1,0:T(8,128)(2,1)} custom-call(bf16[128,2048]{1,0:T(8,128)(2,1)} %tokens.1, s32[1,128]{1,0:T(1,128)} %bitcast.12, s32[1,100]{1,0:T(1,128)} %bitcast.13, f32[4,2048]{1,0:T(4,128)} %group_gain.1, f32[4,2048]{1,0:T(4,128)} %group_b2.1, f32[1,1024]{1,0:T(1,128)} %b1.1, f32[1,2048]{1,0:T(1,128)} %bitcast.9, f32[1,2048]{1,0:T(1,128)} %bitcast.10, ...), custom_call_target="tpu_custom_call" | custom-call | tf_op jit(solution)/shard_map/pallas_call | solution.py:688
  164.0 1.9 %copy.15 = bf16[128,2048]{1,0:T(8,128)(2,1)} copy(bf16[128,2048]{1,0:T(8,128)(2,1)} %shard_map.127) | data formatting | bytes 1048576

commit v6 on v5

--- a/solution.py
+++ b/solution.py
@@ -330,8 +330,15 @@
         pass_on(k, 0, 0, 0)
         pass_on(k, 1, 0, 1)
         between()
-        add_in(k, 0, 0, 0)
-        add_in(k, 1, 0, 1)
+
+    def reduce_alternating(k):
+        for t in (0, 1):
+            for way in (0, 1):
+                add_in(k, way, t + 1, 1 - way)
+            for way in (0, 1):
+                add_in(k, way, t, way)
+        for way in (0, 1):
+            add_in(k, way, 2, way)
 
     returned = {}
 
@@ -540,10 +547,7 @@
     whole("a", 5, 2)
     reduce_start("a", lambda: None)
     drain(8)
-    for t in (1, 2):
-        for c in order:
-            for way in (0, 1):
-                add_in("a", way, t, c)
+    reduce_alternating("a")
 
     gather_start("b")
     for c in order:
@@ -563,6 +567,8 @@
             go_on()
     whole("b", 5, 2)
     reduce_start("b", lambda: go_on(1))
+    add_in("b", 0, 0, 0)
+    add_in("b", 1, 0, 1)
     for t in (1, 2):
         for c in order:
             for way in (0, 1):
@@ -644,6 +650,7 @@
         if q:
             finish_b(q - 1)
     finish_b(quarters - 1)
+    is_late = jnp.sum(spread[...].astype(f32), axis=1, keepdims=True)
     for q in range(quarters):
         cols = quarter(q)
         to_own[q].wait_recv()
@@ -652,8 +659,7 @@
             middle_b[:, cols], spart_b[block_b(0), cols], sown_b[:, cols], ssum_b[:, cols], cols
         ).astype(bf16)
         placed = jnp.dot(spread[...], late_out, preferred_element_type=f32)
-        is_late = jnp.sum(spread[...].astype(f32), axis=1, keepdims=True)
-        encoded[:, cols] = jnp.where(is_late > 0.5, placed, middle[:, cols]).astype(bf16)
+        encoded[:, cols] = jnp.where(is_late > 0.5, placed, middle[:, cols])
     drain(0)
 
 
@@ -687,7 +693,7 @@
 
     return pl.pallas_call(
         fused_kernel,
-        out_shape=jax.ShapeDtypeStruct((count, width), bf16),
+        out_shape=jax.ShapeDtypeStruct((count, width), f32),
         in_specs=[in_vmem] * 9 + [anywhere] * 4,
         out_specs=in_vmem,
         scratch_shapes=[
@@ -755,7 +761,7 @@
         group_w2[0],
         shared_w1,
         shared_w2,
-    )
+    ).astype(bf16)
 
 
 def plain_on_device(

time: 166 us -> 169 us (1.018)
  Pallas kernels: 164 us -> 167 us
  other arithmetic: 0 us -> 2.09 us
  local copies, waits for them, and re-layouts: 1.88 us -> 0 us
    pallas_call x1, Pallas kernels: 164 us -> 167 us  [fused_on_device(): pl.pallas_call(fused_kernel, out_shape=jax.ShapeDtypeStruct((count, width...]
    convert_element_type x0 -> x1, other arithmetic: none -> 2.09 us  [fused_on_device(): return pl.pallas_call(fused_kernel, out_shape=jax.ShapeDtypeStruct((count...]
    unnamed x1 -> x0, local copies, waits for them, and re-layouts: 1.88 us -> none
where the time goes in v6:
time: 169 us
  Pallas kernels  167 us (99%)
  other arithmetic  2.09 us (1%)
    pallas_call x1, Pallas kernels, fused_on_device(): pl.pallas_call(fused_kernel, out_shape=jax.ShapeDtypeStruct((count, width...  167 us

profile of v6, /device:TPU:0, one launch (start us, length us, event | category | flops | bytes accessed | tf_op | source)
XLA Modules:
  0.0 169.1 jit_solution(3384575464102903866)
XLA Ops:
  0.0 167.0 %shard_map.127 = f32[128,2048]{1,0:T(8,128)} custom-call(bf16[128,2048]{1,0:T(8,128)(2,1)} %tokens.1, s32[1,128]{1,0:T(1,128)} %bitcast.12, s32[1,100]{1,0:T(1,128)} %bitcast.13, f32[4,2048]{1,0:T(4,128)} %group_gain.1, f32[4,2048]{1,0:T(4,128)} %group_b2.1, f32[1,1024]{1,0:T(1,128)} %b1.1, f32[1,2048]{1,0:T(1,128)} %bitcast.9, f32[1,2048]{1,0:T(1,128)} %bitcast.10, ...), custom_call_target="tpu_custom_call" | custom-call | tf_op jit(solution)/shard_map/pallas_call | solution.py:694
  167.0 2.1 %convert_element_type.3 = bf16[128,2048]{1,0:T(8,128)(2,1)} convert(f32[128,2048]{1,0:T(8,128)} %shard_map.127) | non-fusion elementwise | flops 262144 | bytes 1572864 | tf_op jit(solution)/shard_map/convert_element_type | solution.py:764

commit v7 on v2

--- a/solution.py
+++ b/solution.py
@@ -206,6 +206,10 @@
         pending.append(copy)
         return copy
 
+    def drain(keep):
+        while len(pending) > keep:
+            pending.pop(0).wait_send()
+
     def chunk(k, slot, c):
         return pl.ds((slot * 4 + c) * caps[k], caps[k])
 
@@ -586,6 +590,7 @@
             sg_recv.at[r, 2],
             peers[r],
         )
+    drain(8)
     near[2].wait_recv()
     near[3] = send(
         sgather_b.at[block_b(2)],
@@ -637,6 +642,7 @@
         if q:
             finish_b(q - 1)
     finish_b(quarters - 1)
+    is_late = jnp.sum(spread[...].astype(f32), axis=1, keepdims=True)
     for q in range(quarters):
         cols = quarter(q)
         to_own[q].wait_recv()
@@ -645,10 +651,8 @@
             middle_b[:, cols], spart_b[block_b(0), cols], sown_b[:, cols], ssum_b[:, cols], cols
         ).astype(bf16)
         placed = jnp.dot(spread[...], late_out, preferred_element_type=f32)
-        is_late = jnp.sum(spread[...].astype(f32), axis=1, keepdims=True)
         encoded[:, cols] = jnp.where(is_late > 0.5, placed, middle[:, cols]).astype(bf16)
-    for copy in pending:
-        copy.wait_send()
+    drain(0)
 
 
 def fused_on_device(

time: 166 us -> 166 us (level)
  no operation moved by 1% of the time
where the time goes in v7:
time: 166 us
  Pallas kernels  164 us (99%)
  local copies, waits for them, and re-layouts  1.88 us (1%)
    pallas_call x1, Pallas kernels, fused_on_device(): pl.pallas_call(fused_kernel, out_shape=jax.ShapeDtypeStruct((count, width...  164 us

profile of v7, /device:TPU:0, one launch (start us, length us, event | category | flops | bytes accessed | tf_op | source)
XLA Modules:
  0.0 165.6 jit_solution(11057624448908694133)
XLA Ops:
  0.0 163.7 %shard_map.127 = bf16[128,2048]{1,0:T(8,128)(2,1)} custom-call(bf16[128,2048]{1,0:T(8,128)(2,1)} %tokens.1, s32[1,128]{1,0:T(1,128)} %bitcast.12, s32[1,100]{1,0:T(1,128)} %bitcast.13, f32[4,2048]{1,0:T(4,128)} %group_gain.1, f32[4,2048]{1,0:T(4,128)} %group_b2.1, f32[1,1024]{1,0:T(1,128)} %b1.1, f32[1,2048]{1,0:T(1,128)} %bitcast.9, f32[1,2048]{1,0:T(1,128)} %bitcast.10, ...), custom_call_target="tpu_custom_call" | custom-call | tf_op jit(solution)/shard_map/pallas_call | solution.py:686
  163.7 1.9 %copy.15 = bf16[128,2048]{1,0:T(8,128)(2,1)} copy(bf16[128,2048]{1,0:T(8,128)(2,1)} %shard_map.127) | data formatting | bytes 1048576
